TPU v7x, 128 devices: a whole 4x4x4 slice. The times are simulated.
128 devices in a mesh: row: 16 (over x_lo, z, core), col: 8 (over x_hi, y).
Axes of the slice: x: 4 (x_hi: 2, x_lo: 2; x = x_hi * 2 + x_lo), y: 4, z: 4, core: 2. Of those that a mesh axis runs over, the one named last changes fastest.
Arguments:
- matrix: bfloat16 [24576, 24576], P('row', 'col'), may hold values from -8 to 8, as said below
- panels: bfloat16 [2, 24576, 128], P(None, 'row'), may hold values from -1 to 1
Outputs:
- updated: bfloat16 [24576, 24576], P('row', 'col')
Inputs may be any that keep to these rules, and one draw needn't show every extreme that they name: matrix is exactly symmetric.
All inputs are finite; a program needn't handle non-finite values.
Results may differ from a plain program's by a relative error of at most 0.015.
Values may be sent and summed in bfloat16 or wider, within the bound.
A program may use at most 128 MiB of HBM per device.

v0:
```python
import jax
import jax.numpy as jnp
from jax import lax
from jax.sharding import PartitionSpec as P

PANELS = 2


def spread(block, axis, source):
    block = jnp.where(lax.axis_index(axis) == source, block, jnp.zeros_like(block))
    return lax.psum(block, axis)


def per_device(matrix, panels):
    row_count = lax.axis_size("row")
    col_count = lax.axis_size("col")
    owner_ratio = row_count // col_count
    row_index = lax.axis_index("row")
    col_index = lax.axis_index("col")
    a_tile = matrix
    n_rows = a_tile.shape[0]
    n_cols = a_tile.shape[1]
    for panel in range(PANELS):
        v_rows = panels[panel]
        gathered = lax.all_gather(v_rows, "row", axis=0, tiled=True)
        v_cols = lax.dynamic_slice_in_dim(gathered, col_index * n_cols, n_cols, 0)
        tile_now = a_tile
        av_fine = lax.psum_scatter(
            lax.dot_general(
                tile_now, v_rows, (((0,), (0,)), ((), ())), preferred_element_type=jnp.float32
            ),
            "row",
            scatter_dimension=0,
            tiled=True,
        )
        av_cols = lax.all_gather(av_fine, "row", axis=0, tiled=True)
        own_rows = lax.dynamic_slice_in_dim(av_cols, row_index % owner_ratio * n_rows, n_rows, 0)
        av_rows = spread(own_rows, "col", row_index // owner_ratio)
        local_sum = jnp.dot(v_rows.astype(jnp.float32).T, av_rows, precision=lax.Precision.HIGHEST)
        curvature = lax.psum(local_sum.astype(jnp.bfloat16), "row").astype(jnp.float32)
        w_cols = (
            av_cols
            - 0.5 * jnp.dot(v_cols.astype(jnp.float32), curvature, precision=lax.Precision.HIGHEST)
        ).astype(jnp.bfloat16)
        w_rows = (
            av_rows
            - 0.5 * jnp.dot(v_rows.astype(jnp.float32), curvature, precision=lax.Precision.HIGHEST)
        ).astype(jnp.bfloat16)
        update = lax.dot_general(
            v_rows, w_cols, (((1,), (1,)), ((), ())), preferred_element_type=jnp.float32
        )
        update = update + lax.dot_general(
            w_rows, v_cols, (((1,), (1,)), ((), ())), preferred_element_type=jnp.float32
        )
        a_tile = (a_tile.astype(jnp.float32) - update).astype(jnp.bfloat16)
    return a_tile


def solution(mesh):
    in_specs = (P("row", "col"), P(None, "row", None))
    out_specs = P("row", "col")
    return jax.shard_map(
        per_device, mesh=mesh, in_specs=in_specs, out_specs=out_specs, check_vma=False
    )
```

profile of v0, /device:TPU:1, one launch (start us, length us, event | category | flops | bytes accessed | tf_op | source)
XLA Modules:
  0.0 567.3 jit_solution(10597587434445006986)
XLA Ops:
  6.5 0.0 copy-start
  6.5 0.0 reduce-scatter.3.cloned.1.call-start
  6.5 7.5 %fusion.34 = f32[3072,128]{1,0:T(8,128)} fusion(bf16[1536,3072]{1,0:T(8,128)(2,1)} %param.2, bf16[2,1536,128]{2,1,0:T(8,128)(2,1)} %param.3), kind=kOutput, calls=%fused_computation.44 | convolution fusion | flops 1207959552 | bytes 11403264 | tf_op jit(solution)/shard_map/dot_general | solution.py:29
  14.1 0.0 reduce-scatter.3.cloned.1.call-update
  14.1 0.0 all-gather.7.cloned.1.call-start
  14.2 62.1 %reduce-scatter.3.cloned.1.call-done = f32[192,128]{1,0:T(8,128)} async-done(((f32[3072,128]{1,0:T(8,128)}), f32[192,128]{1,0:T(8,128)}) %reduce-scatter.3.cloned.1.call-update) | async-done | bytes 98320 | tf_op jit(solution)/shard_map/reduce_scatter | solution.py:28
  76.3 0.0 all-gather.7.cloned.1.call-update
  76.3 0.0 all-reduce.3.cloned.1.call-start
  76.4 37.5 %all-gather.7.cloned.1.call-done = f32[3072,128]{1,0:T(8,128)} async-done(((f32[192,128]{1,0:T(8,128)}), f32[3072,128]{1,0:T(8,128)}) %all-gather.7.cloned.1.call-update) | async-done | bytes 1572880 | tf_op jit(solution)/shard_map/all_gather | solution.py:36
  113.9 2.1 dynamic-slice_select_fusion.1
  115.9 0.0 all-reduce.3.cloned.1.call-update
  116.0 0.0 all-gather.11.cloned.1.call-start
  116.0 0.0 copy-done
  116.0 1.0 fusion.48
  117.0 0.0 all-gather.11.cloned.1.call-update
  117.0 0.0 reduce-scatter.5.cloned.1.call-start
  117.1 0.0 copy-start.1
  117.1 12.7 %copy.3 = bf16[1536,3072]{0,1:T(8,128)(2,1)} copy(bf16[1536,3072]{1,0:T(8,128)(2,1)} %param.2) | data formatting | bytes 18874368 | tf_op args[0]
  129.8 67.8 %all-reduce.3.cloned.1.call-done = f32[1536,128]{1,0:T(8,128)} async-done(((f32[1536,128]{1,0:T(8,128)}), f32[1536,128]{1,0:T(8,128)}) %all-reduce.3.cloned.1.call-update) | async-done | bytes 786448 | tf_op jit(solution)/shard_map/psum | solution.py:11
  197.6 1.9 fusion.14
  199.5 54.5 %psum.29 = bf16[128,128]{0,1:T(8,128)(2,1)S(1)} all-reduce(bf16[128,128]{0,1:T(8,128)(2,1)S(1)} %fusion.14), channel_id=1, replica_groups=mesh['row'=16,'col'=8] {'row'}, use_global_device_ids=true, to_apply=%region_2.3 | all-reduce | flops 16384 | bytes 65536 | tf_op jit(solution)/shard_map/psum | solution.py:40
  254.0 1.4 fusion.13
  255.4 0.0 all-gather.11.cloned.1.call-done
  255.5 0.0 copy-done.1
  255.5 1.5 fusion.6
  257.0 7.9 %fusion.30 = f32[3072,1536]{1,0:T(8,128)} fusion(bf16[3072,128]{1,0:T(8,128)(2,1)S(1)} %fusion.6, bf16[2,1536,128]{2,1,0:T(8,128)(2,1)S(1)} %copy-done), kind=kOutput, calls=%fused_computation.40 | convolution fusion | flops 1207959552 | bytes 20054016 | tf_op jit(solution)/shard_map/dot_general | solution.py:49
  264.9 14.6 %fusion.3 = bf16[1536,3072]{0,1:T(8,128)(2,1)} fusion(f32[3072,1536]{1,0:T(8,128)} %fusion.30, bf16[1536,3072]{0,1:T(8,128)(2,1)} %copy.3, bf16[1536,128]{1,0:T(8,128)(2,1)S(1)} %fusion.13, bf16[1,24576,128]{2,1,0:T(8,128)(2,1)} %all-gather.11.cloned.1.call-done, s32[]{:T(128)S(6)} %select_n.34), kind=kOutput, calls=%fused_computation.5 | convolution fusion | flops 1226833920 | bytes 38928388 | tf_op jit(solution)/shard_map/dot_general | solution.py:52
  279.5 7.4 %fusion.28 = f32[3072,128]{1,0:T(8,128)} fusion(bf16[1536,3072]{0,1:T(8,128)(2,1)} %fusion.3, bf16[2,1536,128]{2,1,0:T(8,128)(2,1)S(1)} %copy-done), kind=kOutput, calls=%fused_computation.38 | convolution fusion | flops 1207959552 | bytes 11403264 | tf_op jit(solution)/shard_map/dot_general | solution.py:29
  286.9 0.0 reduce-scatter.5.cloned.1.call-update
  286.9 0.0 all-gather.9.cloned.1.call-start
  287.0 58.0 %reduce-scatter.5.cloned.1.call-done = f32[192,128]{1,0:T(8,128)} async-done(((f32[3072,128]{1,0:T(8,128)}), f32[192,128]{1,0:T(8,128)}) %reduce-scatter.5.cloned.1.call-update) | async-done | bytes 98320 | tf_op jit(solution)/shard_map/reduce_scatter | solution.py:28
  345.0 0.0 all-gather.9.cloned.1.call-update
  345.0 0.0 all-reduce.5.cloned.1.call-start
  345.0 37.5 %all-gather.9.cloned.1.call-done = f32[3072,128]{1,0:T(8,128)} async-done(((f32[192,128]{1,0:T(8,128)}), f32[3072,128]{1,0:T(8,128)}) %all-gather.9.cloned.1.call-update) | async-done | bytes 1572880 | tf_op jit(solution)/shard_map/all_gather | solution.py:36
  382.6 2.1 dynamic-slice_select_fusion
  384.7 0.0 all-reduce.5.cloned.1.call-update
  384.7 0.0 all-gather.13.cloned.1.call-start
  384.7 0.7 all-gather.13.cloned.1.call-update
  385.4 80.9 %all-reduce.5.cloned.1.call-done = f32[1536,128]{1,0:T(8,128)} async-done(((f32[1536,128]{1,0:T(8,128)}), f32[1536,128]{1,0:T(8,128)}) %all-reduce.5.cloned.1.call-update) | async-done | bytes 786448 | tf_op jit(solution)/shard_map/psum | solution.py:11
  466.3 1.9 fusion.15
  468.2 54.7 %psum.31 = bf16[128,128]{0,1:T(8,128)(2,1)S(1)} all-reduce(bf16[128,128]{0,1:T(8,128)(2,1)S(1)} %fusion.15), channel_id=1, replica_groups=mesh['row'=16,'col'=8] {'row'}, use_global_device_ids=true, to_apply=%region_5.6 | all-reduce | flops 16384 | bytes 65536 | tf_op jit(solution)/shard_map/psum | solution.py:40
  523.0 2.0 fusion.7
  525.0 0.0 copy-start.2
  525.0 7.9 %fusion.24 = f32[3072,1536]{1,0:T(8,128)} fusion(bf16[3072,128]{1,0:T(8,128)(2,1)S(1)} %fusion.7, bf16[2,1536,128]{2,1,0:T(8,128)(2,1)S(1)} %copy-done), kind=kOutput, calls=%fused_computation.34 | convolution fusion | flops 1207959552 | bytes 20054016 | tf_op jit(solution)/shard_map/dot_general | solution.py:49
  532.9 0.0 copy-done.2
  532.9 0.3 fusion.12
  533.2 14.7 %fusion.1 = bf16[1536,3072]{0,1:T(8,128)(2,1)} fusion(f32[3072,1536]{1,0:T(8,128)} %fusion.24, bf16[1536,3072]{0,1:T(8,128)(2,1)} %fusion.3, bf16[1536,128]{1,0:T(8,128)(2,1)S(1)} %fusion.12, bf16[1,24576,128]{2,1,0:T(8,128)(2,1)} %all-gather.13.cloned.1.call-done, s32[]{:T(128)S(6)} %select_n.34), kind=kOutput, calls=%fused_computation.2 | convolution fusion | flops 1226833920 | bytes 38928388 | tf_op jit(solution)/shard_map/dot_general | solution.py:52
  547.9 12.6 %copy.6 = bf16[1536,3072]{1,0:T(8,128)(2,1)} copy(bf16[1536,3072]{0,1:T(8,128)(2,1)} %fusion.1) | data formatting | bytes 18874368 | tf_op jit(solution)/shard_map/convert_element_type | solution.py:55
  (1 shorter events, 0.0 us)
Async XLA Ops:
  6.5 109.5 %copy-start = (bf16[2,1536,128]{2,1,0:T(8,128)(2,1)S(1)}, bf16[2,1536,128]{2,1,0:T(8,128)(2,1)}, u32[]{:S(2)}) copy-start(bf16[2,1536,128]{2,1,0:T(8,128)(2,1)} %param.3) | copy-start | bytes 2359300
  6.5 69.8 %reduce-scatter.3.cloned.1.call-start = ((), (), s32[]{:S(2)}) async-start(), calls=%async_computation.2 | async-start | bytes 1671168 | tf_op jit(solution)/shard_map/reduce_scatter | solution.py:28
  14.1 99.8 %all-gather.7.cloned.1.call-start = ((), (), s32[]{:S(2)}) async-start(), calls=%async_computation.3 | async-start | bytes 1671168 | tf_op jit(solution)/shard_map/all_gather | solution.py:36
  76.3 121.3 %all-reduce.3.cloned.1.call-start = ((), (), s32[]{:S(2)}) async-start(), calls=%async_computation.4 | async-start | bytes 1572864 | tf_op jit(solution)/shard_map/psum | solution.py:11
  116.0 139.5 %all-gather.11.cloned.1.call-start = ((), (), s32[]{:S(2)}) async-start(), calls=%async_computation.8 | async-start | bytes 6684672 | tf_op jit(solution)/shard_map/all_gather | solution.py:25
  117.0 228.0 %reduce-scatter.5.cloned.1.call-start = ((), (), s32[]{:S(2)}) async-start(), calls=%async_computation.5 | async-start | bytes 1671168 | tf_op jit(solution)/shard_map/reduce_scatter | solution.py:28
  117.1 138.4 %copy-start.1 = (f32[3072,128]{1,0:T(8,128)S(1)}, f32[3072,128]{1,0:T(8,128)}, u32[]{:S(2)}) copy-start(f32[3072,128]{1,0:T(8,128)} %all-gather.7.cloned.1.call-done) | copy-start | bytes 4718596
  286.9 95.7 %all-gather.9.cloned.1.call-start = ((), (), s32[]{:S(2)}) async-start(), calls=%async_computation.6 | async-start | bytes 1671168 | tf_op jit(solution)/shard_map/all_gather | solution.py:36
  345.0 121.3 %all-reduce.5.cloned.1.call-start = ((), (), s32[]{:S(2)}) async-start(), calls=%async_computation.7 | async-start | bytes 1572864 | tf_op jit(solution)/shard_map/psum | solution.py:11
  384.7 138.3 %all-gather.13.cloned.1.call-start = ((), (), s32[]{:S(2)}) async-start(), calls=%async_computation.9 | async-start | bytes 6684672 | tf_op jit(solution)/shard_map/all_gather | solution.py:25
  525.0 7.9 %copy-start.2 = (f32[1536,128]{1,0:T(8,128)S(1)}, f32[1536,128]{1,0:T(8,128)}, u32[]{:S(2)}) copy-start(f32[1536,128]{1,0:T(8,128)} %all-reduce.5.cloned.1.call-done) | copy-start | bytes 2359300
Sparse Core Ops, SparseCore 0:
  14.2 62.0 reduce-scatter.2
  78.1 35.7 all-gather.6
  116.5 81.0 all-reduce.2
  199.2 46.1 all-gather.10
  287.1 57.8 reduce-scatter.4
  346.6 35.8 all-gather.8
  385.2 81.0 all-reduce.4
  468.0 46.1 all-gather.12
where the time goes:
time: 571 us; the launch traced here: 567 us
  waiting for transfers between devices  345 us (60%)
  blocking collectives  109 us (19%)
  matrix products  69.1 us (12%)
  local copies, waits for them, and re-layouts  26.3 us (5%)
  between operations  13.6 us (2%)
    psum x2, waiting for transfers between devices, spread(): return lax.psum(block, axis)  149 us
    reduce_scatter x2, waiting for transfers between devices, per_device(): lax.psum_scatter(lax.dot_general(tile_now, v_rows, (((0,), (0,)), ((), ()...  120 us
    psum x2, blocking collectives, per_device(): lax.psum(local_sum.astype(jnp.bfloat16), 'row').astype(jnp.float32)  109 us
    all_gather x2, waiting for transfers between devices, per_device(): av_cols = lax.all_gather(av_fine, 'row', axis=0, tiled=True)  75 us
    dot_general x2, matrix products, per_device(): lax.dot_general(w_rows, v_cols, (((1,), (1,)), ((), ())), preferred_eleme...  29.3 us
    dot_general x2, matrix products, per_device(): lax.dot_general(v_rows, w_cols, (((1,), (1,)), ((), ())), preferred_eleme...  15.8 us
    dot_general x2, matrix products, per_device(): lax.dot_general(tile_now, v_rows, (((0,), (0,)), ((), ())), preferred_ele...  15 us
    unnamed x7, local copies, waits for them, and re-layouts  12.7 us
  transfers between devices with their start and end apart: 8, of which 6 were waited for; matrix products, arithmetic and copies ran while one was open for 3% of the time, Pallas kernels for 0%

commit v1 on v0

v1 whole, which is shorter than its diff:
```python
import functools

import jax
import jax.numpy as jnp
from jax import lax
from jax.experimental import pallas as pl
from jax.experimental.pallas import tpu as pltpu
from jax.sharding import PartitionSpec as P

MESH = pl.DeviceIdType.MESH
F32 = jnp.float32
BF16 = jnp.bfloat16

ROWS = 1536
HALVES = 2
WIDE = 256
SUB = 4
SUBW = ROWS // SUB
PIECE = 32
CROWS = PIECE + 16
NN = (((1,), (0,)), ((), ()))
NT = (((1,), (1,)), ((), ()))
TN = (((0,), (0,)), ((), ()))


def dot(a, b, dims, precision=None):
    return lax.dot_general(a, b, dims, preferred_element_type=F32, precision=precision)


def exchange_kernel(
    a_ref, v_ref, x_ref, y_ref,
    a_buf, vt, q_send, q_own, sib_in, x_send, x_own, x_in, z_send, z_in, piece, vpiece,
    turned, prt, c_send, c_sib, c_half, c_col, c_row, c_full,
    a_sem, s_send, s_recv,
):
    row = lax.axis_index("row")
    col = lax.axis_index("col")
    core = row % 2
    big = row // 2
    z = big % 4
    xl = big // 4

    sibling = (big * 2 + 1 - core, col)

    def row_peer(j):
        other = (xl + j // 4) % 2 * 4 + (z + j % 4) % 4
        return other, (other * 2 + core, col)

    def col_peer(j):
        other = (col // 4 + j // 4) % 2 * 4 + (col % 4 + j % 4) % 4
        return other, (row, other)

    mirror = (col * 2 + core, big)
    on_diagonal = big == col

    used = [0]

    def copy(src, dst, to):
        i = used[0]
        used[0] += 1
        return pltpu.make_async_remote_copy(
            src_ref=src, dst_ref=dst, send_sem=s_send.at[i], recv_sem=s_recv.at[i],
            device_id=to, device_id_type=MESH,
        )

    loads = []
    for s in range(SUB):
        for h in range(HALVES):
            half = 1 - core if h == 0 else core
            start = pl.multiple_of(half * ROWS + s * SUBW, 128)
            loads.append(
                pltpu.make_async_copy(a_ref.at[:, pl.ds(start, SUBW)], a_buf.at[2 * s + h], a_sem.at[2 * s + h])
            )
    for load in loads:
        load.start()

    barrier = pltpu.get_barrier_semaphore()
    pl.semaphore_signal(barrier, inc=1, device_id=sibling, device_id_type=MESH)
    for j in range(1, 8):
        pl.semaphore_signal(barrier, inc=1, device_id=row_peer(j)[1], device_id_type=MESH)
        pl.semaphore_signal(barrier, inc=1, device_id=col_peer(j)[1], device_id_type=MESH)

    @pl.when(jnp.logical_not(on_diagonal))
    def _():
        pl.semaphore_signal(barrier, inc=1, device_id=mirror, device_id_type=MESH)

    vt[:128, :] = v_ref[0].T
    vt[128:, :] = v_ref[1].T

    @pl.when(on_diagonal)
    def _():
        pl.semaphore_wait(barrier, 15)

    @pl.when(jnp.logical_not(on_diagonal))
    def _():
        pl.semaphore_wait(barrier, 16)

    v_turn = copy(vt.at[pl.ds(pl.multiple_of(col * PIECE, PIECE), PIECE)], vpiece, mirror)

    @pl.when(jnp.logical_not(on_diagonal))
    def _():
        v_turn.start()

    @pl.when(on_diagonal)
    def _():
        vpiece[...] = vt[pl.ds(pl.multiple_of(col * PIECE, PIECE), PIECE), :]

    sib = []
    for s in range(SUB):
        loads[2 * s].wait()
        q_send[s] = dot(vt[...], a_buf[2 * s], NN).astype(BF16)
        sib.append(copy(q_send.at[s], sib_in.at[s], sibling))
        sib[s].start()
        loads[2 * s + 1].wait()
        q_own[s] = dot(vt[...], a_buf[2 * s + 1], NN)

    mine = pl.multiple_of(big * PIECE, PIECE)
    my_half = pl.multiple_of(core * ROWS, ROWS)
    @pl.when(jnp.logical_not(on_diagonal))
    def _():
        v_turn.wait()
    y_ref[pl.ds(WIDE + mine, PIECE), pl.ds(my_half, ROWS)] = vpiece[...]
    v_gather = []
    for j in range(1, 8):
        c = copy(vpiece, y_ref.at[pl.ds(WIDE + mine, PIECE), pl.ds(my_half, ROWS)], row_peer(j)[1])
        c.start()
        v_gather.append(c)

    other_x = ((1 - xl) * 4 + z) * 2 + core
    xs = []
    for s in range(SUB):
        sib[s].wait_recv()
        x_send[s] = (
            q_own[s, pl.ds(pl.multiple_of((1 - xl) * 128, 128), 128)]
            + sib_in[s, pl.ds(pl.multiple_of((1 - xl) * 128, 128), 128)].astype(F32)
        ).astype(BF16)
        xs.append(copy(x_send.at[s], x_in.at[s], (other_x, col)))
        xs[s].start()
        x_own[s] = q_own[s, pl.ds(pl.multiple_of(xl * 128, 128), 128)] + sib_in[
            s, pl.ds(pl.multiple_of(xl * 128, 128), 128)
        ].astype(F32)
    zs = []
    for s in range(SUB):
        xs[s].wait_recv()
        x_own[s] = x_own[s] + x_in[s].astype(F32)
        z_send[s] = x_own[s].astype(BF16)
        for j in range(1, 4):
            to = (z + j) % 4
            c = copy(
                z_send.at[s, pl.ds(pl.multiple_of(to * PIECE, PIECE), PIECE)],
                z_in.at[s, j - 1],
                ((xl * 4 + to) * 2 + core, col),
            )
            c.start()
            zs.append(c)
    for s in range(SUB):
        total = x_own[s, pl.ds(pl.multiple_of(z * PIECE, PIECE), PIECE)]
        for j in range(3):
            zs[3 * s + j].wait_recv()
            total = total + z_in[s, j].astype(F32)
        piece[:, s * SUBW:(s + 1) * SUBW] = total.astype(BF16)

    p_turn = copy(piece, turned, mirror)

    @pl.when(jnp.logical_not(on_diagonal))
    def _():
        p_turn.start()

    @pl.when(on_diagonal)
    def _():
        turned[...] = piece[...]

    p_gather = []
    for j in range(1, 8):
        c = copy(piece, y_ref.at[pl.ds(mine, PIECE), pl.ds(my_half, ROWS)], row_peer(j)[1])
        c.start()
        p_gather.append(c)
    y_ref[pl.ds(mine, PIECE), pl.ds(my_half, ROWS)] = piece[...]

    for c in v_gather:
        c.wait_recv()
    v_share = copy(
        y_ref.at[pl.ds(WIDE, WIDE), pl.ds(my_half, ROWS)],
        y_ref.at[pl.ds(WIDE, WIDE), pl.ds(my_half, ROWS)], sibling,
    )
    v_share.start()

    v_half = y_ref[pl.ds(WIDE, WIDE), pl.ds(my_half, ROWS)]
    c_send[:PIECE, :] = dot(piece[...], v_half, NT)
    c_send[PIECE:, :] = dot(
        y_ref[pl.ds(pl.multiple_of(WIDE + big * 16, 16), 16), pl.ds(my_half, ROWS)], v_half, NT
    )
    hrows = CROWS // 2
    c_pair = copy(c_send.at[pl.ds(pl.multiple_of((1 - core) * hrows, 8), hrows)], c_sib, sibling)
    c_pair.start()

    @pl.when(jnp.logical_not(on_diagonal))
    def _():
        p_turn.wait()
    mine_r = pl.multiple_of(col * PIECE, PIECE)
    prt[pl.ds(mine_r, PIECE), :] = turned[...]
    r_gather = []
    for j in range(1, 8):
        c = copy(turned, prt.at[pl.ds(mine_r, PIECE)], col_peer(j)[1])
        c.start()
        r_gather.append(c)

    c_pair.wait_recv()
    c_half[...] = c_send[pl.ds(pl.multiple_of(core * hrows, 8), hrows), :] + c_sib[...]
    cc = []
    for j in range(1, 8):
        c = copy(c_half, c_col.at[j - 1], col_peer(j)[1])
        c.start()
        cc.append(c)
    total = c_half[...]
    for j in range(7):
        cc[j].wait_recv()
        total = total + c_col[j]
    c_row[...] = total
    slot = big * 2 + core
    cr = []
    for j in range(1, 8):
        c = copy(c_row, c_full.at[slot], row_peer(j)[1])
        c.start()
        cr.append(c)
    c = copy(c_row, c_full.at[slot], sibling)
    c.start()
    cr.append(c)
    c_full[slot] = c_row[...]
    for c in cr:
        c.wait_recv()
    fwd = []
    for j in range(1, 8):
        other = row_peer(j)[0] * 2 + core
        c = copy(c_full.at[other], c_full.at[other], sibling)
        c.start()
        fwd.append(c)
    for c in fwd:
        c.wait_recv()

    crows = [jnp.concatenate([c_full[2 * i], c_full[2 * i + 1]], axis=0) for i in range(8)]
    cpv = jnp.concatenate([m[:PIECE] for m in crows], axis=0)
    g01 = jnp.concatenate([m[PIECE:, 128:] for m in crows], axis=0)
    hi = lax.Precision.HIGHEST
    c00 = cpv[:128, :128]
    c01 = cpv[:128, 128:]
    c11 = cpv[128:, 128:]
    d = c01 - dot(c00, g01, NN, hi)
    curv = c11 - dot(c01, g01, TN, hi) - dot(g01, d, TN, hi)
    t2 = -jnp.concatenate(
        [jnp.concatenate([c00, d], axis=1), jnp.concatenate([d.T, curv], axis=1)], axis=0
    )
    t2b = t2.astype(BF16)
    g01b = g01.astype(BF16)

    v0 = v_ref[0]
    v1 = v_ref[1]
    x_ref[:, :128] = (v0.astype(F32) - dot(v1, g01b, NT)).astype(BF16)
    x_ref[:, 128:256] = v1
    vt2 = dot(v0, t2b[:128], NN) + dot(v1, t2b[128:], NN)

    for c in p_gather:
        c.wait_recv()
    p_share = copy(
        y_ref.at[pl.ds(0, WIDE), pl.ds(my_half, ROWS)],
        y_ref.at[pl.ds(0, WIDE), pl.ds(my_half, ROWS)], sibling,
    )
    p_share.start()
    for c in r_gather:
        c.wait_recv()
    p0 = prt[:128, :].T
    p1 = prt[128:, :].T
    x_ref[:, 256:384] = (vt2[:, :128] + p0.astype(F32)).astype(BF16)
    x_ref[:, 384:] = (vt2[:, 128:] + p1.astype(F32) - dot(p0, g01b, NN)).astype(BF16)

    for c in sib + v_gather + xs + zs + p_gather + [c_pair] + r_gather + cc + cr + fwd:
        c.wait_send()
    v_share.wait()
    p_share.wait()


N_COPIES = 1 + SUB + 7 + SUB + 3 * SUB + 1 + 7 + 1 + 1 + 7 + 7 + 8 + 7 + 1


def exchange(matrix, panels):
    return pl.pallas_call(
        exchange_kernel,
        out_shape=(
            jax.ShapeDtypeStruct((ROWS, 2 * WIDE), BF16),
            jax.ShapeDtypeStruct((2 * WIDE, 2 * ROWS), BF16),
        ),
        in_specs=[pl.BlockSpec(memory_space=pl.ANY), pl.BlockSpec(memory_space=pltpu.VMEM)],
        out_specs=(pl.BlockSpec(memory_space=pltpu.VMEM), pl.BlockSpec(memory_space=pltpu.VMEM)),
        scratch_shapes=[
            pltpu.VMEM((2 * SUB, ROWS, SUBW), BF16),
            pltpu.VMEM((WIDE, ROWS), BF16),
            pltpu.VMEM((SUB, WIDE, SUBW), BF16),
            pltpu.VMEM((SUB, WIDE, SUBW), F32),
            pltpu.VMEM((SUB, WIDE, SUBW), BF16),
            pltpu.VMEM((SUB, 128, SUBW), BF16),
            pltpu.VMEM((SUB, 128, SUBW), F32),
            pltpu.VMEM((SUB, 128, SUBW), BF16),
            pltpu.VMEM((SUB, 128, SUBW), BF16),
            pltpu.VMEM((SUB, 3, PIECE, SUBW), BF16),
            pltpu.VMEM((PIECE, ROWS), BF16),
            pltpu.VMEM((PIECE, ROWS), BF16),
            pltpu.VMEM((PIECE, ROWS), BF16),
            pltpu.VMEM((WIDE, ROWS), BF16),
            pltpu.VMEM((CROWS, WIDE), F32),
            pltpu.VMEM((CROWS // 2, WIDE), F32),
            pltpu.VMEM((CROWS // 2, WIDE), F32),
            pltpu.VMEM((7, CROWS // 2, WIDE), F32),
            pltpu.VMEM((CROWS // 2, WIDE), F32),
            pltpu.VMEM((16, CROWS // 2, WIDE), F32),
            pltpu.SemaphoreType.DMA((2 * SUB,)),
            pltpu.SemaphoreType.DMA((N_COPIES,)),
            pltpu.SemaphoreType.DMA((N_COPIES,)),
        ],
        compiler_params=pltpu.CompilerParams(
            collective_id=0, has_side_effects=True, vmem_limit_bytes=48 * 2**20
        ),
        name="exchange",
    )(matrix, panels)


def update_kernel(a_ref, x_ref, y_ref, o_ref):
    o_ref[...] = (a_ref[...].astype(F32) - dot(x_ref[...], y_ref[...], NN)).astype(BF16)


def update(matrix, x, y):
    block = 256
    return pl.pallas_call(
        update_kernel,
        out_shape=jax.ShapeDtypeStruct(matrix.shape, BF16),
        grid=(matrix.shape[1] // block,),
        in_specs=[
            pl.BlockSpec((ROWS, block), lambda i: (0, i)),
            pl.BlockSpec((ROWS, 2 * WIDE), lambda i: (0, 0)),
            pl.BlockSpec((2 * WIDE, block), lambda i: (0, i)),
        ],
        out_specs=pl.BlockSpec((ROWS, block), lambda i: (0, i)),
        compiler_params=pltpu.CompilerParams(vmem_limit_bytes=48 * 2**20),
        name="update",
    )(matrix, x, y)


def per_device(matrix, panels):
    x, y = exchange(matrix, panels)
    return update(matrix, x, y)


def solution(mesh):
    return jax.shard_map(
        per_device,
        mesh=mesh,
        in_specs=(P("row", "col"), P(None, "row", None)),
        out_specs=P("row", "col"),
        check_vma=False,
    )
```

time: 571 us -> 84.8 us (0.15)
  waiting for transfers between devices: 345 us -> 0 us
  blocking collectives: 109 us -> 0 us
  Pallas kernels: 0 us -> 83.2 us
  matrix products: 69.1 us -> 0 us
  local copies, waits for them, and re-layouts: 26.3 us -> 1.13 us
  between operations: 13.6 us -> 0.01 us
    psum x2 -> x0, waiting for transfers between devices: 149 us -> none  [spread(): return lax.psum(block, axis)]
    reduce_scatter x2 -> x0, waiting for transfers between devices: 120 us -> none  [per_device(): lax.psum_scatter(lax.dot_general(tile_now, v_rows, (((0,), (0,)), ((), ()...]
    psum x2 -> x0, blocking collectives: 109 us -> none  [per_device(): lax.psum(local_sum.astype(jnp.bfloat16), 'row').astype(jnp.float32)]
    pallas_call x0 -> x2, Pallas kernels: none -> 83.2 us  [the longest x1 69.7 us: exchange(): pl.pallas_call(exchange_kernel, out_shape=(jax.ShapeDtypeStruct((ROWS, 2...]
    all_gather x4 -> x0, waiting for transfers between devices: 75 us -> none  [the longest x2 75 us: per_device(): av_cols = lax.all_gather(av_fine, 'row', axis=0, tiled=True)]
    dot_general x12 -> x0, matrix products: 69.1 us -> none  [the longest x2 29.3 us: per_device(): lax.dot_general(w_rows, v_cols, (((1,), (1,)), ((), ())), preferred_eleme...]
    convert_element_type x1 -> x0, local copies, waits for them, and re-layouts: 12.6 us -> none  [per_device(): a_tile = (a_tile.astype(jnp.float32) - update).astype(jnp.bfloat16)]
    unnamed x7 -> x2, local copies, waits for them, and re-layouts: 12.7 us -> 1.13 us
  transfers between devices with their start and end apart: 8 -> 0, of which waited for: 6 -> 0; matrix products, arithmetic and copies ran while one was open for 3% -> 0% of each run, Pallas kernels for 0% -> 0%
where the time goes in v1:
time: 84.8 us; the launch traced here: 84.4 us
  Pallas kernels  83.2 us (98%)
  local copies, waits for them, and re-layouts  1.13 us (1%)
    pallas_call x1, Pallas kernels, exchange(): pl.pallas_call(exchange_kernel, out_shape=(jax.ShapeDtypeStruct((ROWS, 2...  69.7 us
    pallas_call x1, Pallas kernels, update(): pl.pallas_call(update_kernel, out_shape=jax.ShapeDtypeStruct(matrix.shape...  13.5 us

profile of v1, /device:TPU:1, one launch (start us, length us, event | category | flops | bytes accessed | tf_op | source)
XLA Modules:
  0.0 84.4 jit_solution(5957942340151116084)
XLA Ops:
  0.0 0.0 copy-start
  0.0 1.1 %copy-done = bf16[2,1536,128]{2,1,0:T(8,128)(2,1)S(1)} copy-done((bf16[2,1536,128]{2,1,0:T(8,128)(2,1)S(1)}, bf16[2,1536,128]{2,1,0:T(8,128)(2,1)}, u32[]{:S(2)}) %copy-start) | copy-done | bytes 786456
  1.1 69.7 %exchange.1 = (bf16[1536,512]{1,0:T(8,128)(2,1)S(1)}, bf16[512,3072]{1,0:T(8,128)(2,1)S(1)}) custom-call(bf16[1536,3072]{1,0:T(8,128)(2,1)} %a_ref.3, bf16[2,1536,128]{2,1,0:T(8,128)(2,1)S(1)} %copy-done), custom_call_target="tpu_custom_call" | custom-call | tf_op jit(solution)/shard_map/exchange/pallas_call | solution.py:286
  70.9 13.5 %update.1 = bf16[1536,3072]{1,0:T(8,128)(2,1)} custom-call(bf16[1536,3072]{1,0:T(8,128)(2,1)} %a_ref.3, bf16[1536,512]{1,0:T(8,128)(2,1)S(1)} %get-tuple-element.7.x_ref, bf16[512,3072]{1,0:T(8,128)(2,1)S(1)} %get-tuple-element.8.y_ref), custom_call_target="tpu_custom_call" | custom-call | tf_op jit(solution)/shard_map/update/pallas_call | solution.py:332
Async XLA Ops:
  0.0 1.1 %copy-start = (bf16[2,1536,128]{2,1,0:T(8,128)(2,1)S(1)}, bf16[2,1536,128]{2,1,0:T(8,128)(2,1)}, u32[]{:S(2)}) copy-start(bf16[2,1536,128]{2,1,0:T(8,128)(2,1)} %v_ref.1) | copy-start | bytes 2359300

commit v2 on v0

v2 whole, which is shorter than its diff:
```python
import jax
import jax.numpy as jnp
from jax import lax
from jax.experimental import pallas as pl
from jax.experimental.pallas import tpu as pltpu
from jax.sharding import PartitionSpec as P

MESH = pl.DeviceIdType.MESH
F32 = jnp.float32
BF16 = jnp.bfloat16

ROWS = 1536
WIDE = 256
SUB = 3
SUBW = ROWS // SUB
BLOCKS = 2 * SUB
PIECE = 32
CROWS = PIECE + 16
AHEAD = 3
NN = (((1,), (0,)), ((), ()))
NT = (((1,), (1,)), ((), ()))
TN = (((0,), (0,)), ((), ()))


def dot(a, b, dims, precision=None):
    return lax.dot_general(a, b, dims, preferred_element_type=F32, precision=precision)


def exchange_kernel(
    a_ref, v_ref, a_out, x_ref, y_ref,
    vt, q_send, q_own, sib_in, x_send, x_in, z_send, z_in, zz_in, xx_send, xx_in,
    prt, c_send, c_col, c_full, c_sib,
    a_sem, s_send, s_recv,
):
    row = lax.axis_index("row")
    col = lax.axis_index("col")
    core = row % 2
    big = row // 2
    z = big % 4
    xl = big // 4
    yy = col % 4
    xh = col // 4

    sibling = (big * 2 + 1 - core, col)
    x_peer = (((1 - xl) * 4 + z) * 2 + core, col)
    z_peers = [((xl * 4 + (z + j) % 4) * 2 + core, col) for j in range(1, 4)]
    h_peer = (row, (1 - xh) * 4 + yy)
    y_peers = [(row, xh * 4 + (yy + j) % 4) for j in range(1, 4)]
    row_peers = [x_peer] + z_peers + [(((1 - xl) * 4 + (z + j) % 4) * 2 + core, col) for j in range(1, 4)]
    col_peers = [h_peer] + y_peers + [(row, (1 - xh) * 4 + (yy + j) % 4) for j in range(1, 4)]
    mirror = (col * 2 + core, big)
    on_diagonal = big == col
    off_diagonal = jnp.logical_not(on_diagonal)

    used = [0]
    sent = []

    def copy(src, dst, to):
        i = used[0]
        used[0] += 1
        return pltpu.make_async_remote_copy(
            src_ref=src, dst_ref=dst, send_sem=s_send.at[i], recv_sem=s_recv.at[i],
            device_id=to, device_id_type=MESH,
        )

    def send(src, dst, to):
        c = copy(src, dst, to)
        c.start()
        sent.append(c)
        return c

    loads = []
    for i in range(BLOCKS):
        b = (1 - core if i % 2 == 0 else core) * SUB + i // 2
        start = pl.multiple_of(b * SUBW, 128)
        loads.append((b, pltpu.make_async_copy(a_ref.at[:, pl.ds(start, SUBW)], a_out.at[b], a_sem.at[i])))
    for _, load in loads[:AHEAD]:
        load.start()

    barrier = pltpu.get_barrier_semaphore()
    for peer in [sibling] + row_peers + col_peers:
        pl.semaphore_signal(barrier, inc=1, device_id=peer, device_id_type=MESH)

    @pl.when(off_diagonal)
    def _():
        pl.semaphore_signal(barrier, inc=1, device_id=mirror, device_id_type=MESH)

    vt[:128, :] = v_ref[0].T
    vt[128:, :] = v_ref[1].T

    mine = pl.multiple_of(big * PIECE, PIECE)
    mine_v = pl.multiple_of(WIDE + big * PIECE, PIECE)
    mine_r = pl.multiple_of(col * PIECE, PIECE)
    half = pl.multiple_of(core * ROWS, ROWS)
    v_turn = copy(
        vt.at[pl.ds(mine_r, PIECE)],
        y_ref.at[pl.ds(pl.multiple_of(WIDE + col * PIECE, PIECE), PIECE), pl.ds(half, ROWS)],
        mirror,
    )

    sib = []
    for i, (b, load) in enumerate(loads):
        load.wait()
        if i + AHEAD < BLOCKS:
            loads[i + AHEAD][1].start()
        part = dot(vt[...], a_out[b], NN).reshape(2, 4, PIECE, SUBW)
        if i == 0:

            @pl.when(on_diagonal)
            def _():
                pl.semaphore_wait(barrier, 15)
                y_ref[pl.ds(mine_v, PIECE), pl.ds(half, ROWS)] = vt[pl.ds(mine_r, PIECE), :]

            @pl.when(off_diagonal)
            def _():
                pl.semaphore_wait(barrier, 16)
                v_turn.start()

        if i % 2 == 0:
            q_send[i // 2] = part.astype(BF16)
            sib.append(send(q_send.at[i // 2], sib_in.at[i // 2], sibling))
        else:
            q_own[i // 2] = part

    sib[0].wait_recv()
    q_own[0] = q_own[0] + sib_in[0].astype(F32)
    q_send_z = z_send.at[0]
    q_send_z[...] = q_own[0].astype(BF16)
    zz = [send(q_send_z.at[:, (z + j) % 4], zz_in.at[j - 1], z_peers[j - 1]) for j in range(1, 4)]
    xs = [None]
    for s in range(1, SUB):
        sib[s].wait_recv()
        x_send[s - 1] = (q_own[s, 1 - xl] + sib_in[s, 1 - xl].astype(F32)).astype(BF16)
        xs.append(send(x_send.at[s - 1], x_in.at[s - 1], x_peer))
        q_own[s, xl] = q_own[s, xl] + sib_in[s, xl].astype(F32)

    @pl.when(off_diagonal)
    def _():
        v_turn.wait()

    v_place = y_ref.at[pl.ds(mine_v, PIECE), pl.ds(half, ROWS)]
    v_x = send(v_place, v_place, x_peer)
    v_wait = [send(v_place, v_place, p) for p in z_peers]

    for c in zz:
        c.wait_recv()
    total = q_own[0, :, z]
    for j in range(3):
        total = total + zz_in[j].astype(F32)
    q_own[0, :, z] = total
    xx_send[...] = q_own[0, 1 - xl, z].astype(BF16)
    xx = send(xx_send, xx_in, x_peer)

    zs = [None]
    for s in range(1, SUB):
        xs[s].wait_recv()
        total = q_own[s, xl] + x_in[s - 1].astype(F32)
        q_own[s, xl] = total
        z_send[s, 0] = total.astype(BF16)
        zs.append(
            [send(z_send.at[s, 0, (z + j) % 4], z_in.at[s - 1, j - 1], z_peers[j - 1]) for j in range(1, 4)]
        )

    v_x.wait_recv()
    other_v = pl.multiple_of(WIDE + ((1 - xl) * 4 + z) * PIECE, PIECE)
    v_place2 = y_ref.at[pl.ds(other_v, PIECE), pl.ds(half, ROWS)]
    v_wait += [send(v_place2, v_place2, p) for p in z_peers]

    turns = []
    p_x = []
    p_wait = [[] for _ in range(SUB)]
    for s in range(SUB):
        if s == 0:
            xx.wait_recv()
            total = q_own[0, xl, z] + xx_in[...].astype(F32)
        else:
            total = q_own[s, xl, z]
            for j in range(3):
                zs[s][j].wait_recv()
                total = total + z_in[s - 1, j].astype(F32)
        columns = pl.ds(pl.multiple_of(core * ROWS + s * SUBW, 128), SUBW)
        place = y_ref.at[pl.ds(mine, PIECE), columns]
        place[...] = total.astype(BF16)
        turn = copy(place, prt.at[pl.ds(mine, PIECE), pl.ds(s * SUBW, SUBW)], mirror)
        turns.append(turn)

        @pl.when(off_diagonal)
        def _():
            turn.start()

        @pl.when(on_diagonal)
        def _():
            prt[pl.ds(mine, PIECE), pl.ds(s * SUBW, SUBW)] = place[...]

        p_x.append(send(place, place, x_peer))
        p_wait[s] += [send(place, place, p) for p in z_peers]

    for c in v_wait:
        c.wait_recv()
    v_place = y_ref.at[pl.ds(WIDE, WIDE), pl.ds(half, ROWS)]
    v_share = send(v_place, v_place, sibling)
    v_half = v_place[...]
    c_send[0, :PIECE, :] = dot(y_ref[pl.ds(mine, PIECE), pl.ds(half, ROWS)], v_half, NT)
    c_send[0, PIECE:, :] = dot(
        y_ref[pl.ds(pl.multiple_of(WIDE + big * 16, 16), 16), pl.ds(half, ROWS)], v_half, NT
    )
    c_full[16] = c_send[0].astype(BF16)
    cc = [send(c_full.at[16], c_col.at[j], p) for j, p in enumerate(col_peers)]

    r_x = []
    r_wait = [[] for _ in range(SUB)]
    for s in range(SUB):

        @pl.when(off_diagonal)
        def _():
            turns[s].wait()

        place = prt.at[pl.ds(mine_r, PIECE), pl.ds(s * SUBW, SUBW)]
        r_x.append(send(place, place, h_peer))
        r_wait[s] += [send(place, place, p) for p in y_peers]

    other_p = pl.multiple_of(((1 - xl) * 4 + z) * PIECE, PIECE)
    for s in range(SUB):
        p_x[s].wait_recv()
        place = y_ref.at[pl.ds(other_p, PIECE), pl.ds(pl.multiple_of(core * ROWS + s * SUBW, 128), SUBW)]
        p_wait[s] += [send(place, place, p) for p in z_peers]

    total = c_send[0]
    for j in range(7):
        cc[j].wait_recv()
        total = total + c_col[j].astype(F32)
    c_full[core * 8 + big] = total.astype(BF16)
    place = c_full.at[core * 8 + big]
    cr = [send(place, place, p) for p in row_peers]

    other_r = pl.multiple_of(((1 - xh) * 4 + yy) * PIECE, PIECE)
    for s in range(SUB):
        r_x[s].wait_recv()
        place = prt.at[pl.ds(other_r, PIECE), pl.ds(s * SUBW, SUBW)]
        r_wait[s] += [send(place, place, p) for p in y_peers]

    for c in cr:
        c.wait_recv()
    place = c_full.at[pl.ds(pl.multiple_of(core * 8, 8), 8)]
    c_share = send(place, c_sib, sibling)
    c_share.wait_recv()

    crows = [c_full[core * 8 + i].astype(F32) + c_sib[i].astype(F32) for i in range(8)]
    cpv = jnp.concatenate([m[:PIECE] for m in crows], axis=0)
    g01 = jnp.concatenate([m[PIECE:, 128:] for m in crows], axis=0)
    hi = lax.Precision.HIGHEST
    c00 = cpv[:128, :128]
    c01 = cpv[:128, 128:]
    c11 = cpv[128:, 128:]
    d = c01 - dot(c00, g01, NN, hi)
    curv = c11 - dot(c01, g01, TN, hi) - dot(g01, d, TN, hi)
    t2 = -jnp.concatenate(
        [jnp.concatenate([c00, d], axis=1), jnp.concatenate([d.T, curv], axis=1)], axis=0
    )
    t2b = t2.astype(BF16)
    g01b = g01.astype(BF16)

    p_share = []
    for s in range(SUB):
        for c in p_wait[s]:
            c.wait_recv()
        place = y_ref.at[pl.ds(0, WIDE), pl.ds(pl.multiple_of(core * ROWS + s * SUBW, 128), SUBW)]
        p_share.append(send(place, place, sibling))

    for s in range(SUB):
        rows = slice(s * SUBW, (s + 1) * SUBW)
        v0 = v_ref[0, rows]
        v1 = v_ref[1, rows]
        x_ref[rows, :128] = (v0.astype(F32) - dot(v1, g01b, NT)).astype(BF16)
        x_ref[rows, 128:256] = v1
        vt2 = dot(v0, t2b[:128], NN) + dot(v1, t2b[128:], NN)
        for c in r_wait[s]:
            c.wait_recv()
        p0 = prt[:128, rows].T
        p1 = prt[128:, rows].T
        x_ref[rows, 256:384] = (vt2[:, :128] + p0.astype(F32)).astype(BF16)
        x_ref[rows, 384:] = (vt2[:, 128:] + p1.astype(F32) - dot(p0, g01b, NN)).astype(BF16)

    v_share.wait_recv()
    for c in p_share:
        c.wait_recv()
    for c in sent:
        c.wait_send()


N_COPIES = 160


def exchange(matrix, panels):
    return pl.pallas_call(
        exchange_kernel,
        out_shape=(
            jax.ShapeDtypeStruct((BLOCKS, ROWS, SUBW), BF16),
            jax.ShapeDtypeStruct((ROWS, 2 * WIDE), BF16),
            jax.ShapeDtypeStruct((2 * WIDE, 2 * ROWS), BF16),
        ),
        in_specs=[pl.BlockSpec(memory_space=pl.ANY), pl.BlockSpec(memory_space=pltpu.VMEM)],
        out_specs=(pl.BlockSpec(memory_space=pltpu.VMEM),) * 3,
        scratch_shapes=[
            pltpu.VMEM((WIDE, ROWS), BF16),
            pltpu.VMEM((SUB, 2, 4, PIECE, SUBW), BF16),
            pltpu.VMEM((SUB, 2, 4, PIECE, SUBW), F32),
            pltpu.VMEM((SUB, 2, 4, PIECE, SUBW), BF16),
            pltpu.VMEM((SUB - 1, 4, PIECE, SUBW), BF16),
            pltpu.VMEM((SUB - 1, 4, PIECE, SUBW), BF16),
            pltpu.VMEM((SUB, 2, 4, PIECE, SUBW), BF16),
            pltpu.VMEM((SUB - 1, 3, PIECE, SUBW), BF16),
            pltpu.VMEM((3, 2, PIECE, SUBW), BF16),
            pltpu.VMEM((PIECE, SUBW), BF16),
            pltpu.VMEM((PIECE, SUBW), BF16),
            pltpu.VMEM((WIDE, ROWS), BF16),
            pltpu.VMEM((1, CROWS, WIDE), F32),
            pltpu.VMEM((7, CROWS, WIDE), BF16),
            pltpu.VMEM((17, CROWS, WIDE), BF16),
            pltpu.VMEM((8, CROWS, WIDE), BF16),
            pltpu.SemaphoreType.DMA((BLOCKS,)),
            pltpu.SemaphoreType.DMA((N_COPIES,)),
            pltpu.SemaphoreType.DMA((N_COPIES,)),
        ],
        compiler_params=pltpu.CompilerParams(
            collective_id=0, has_side_effects=True, vmem_limit_bytes=36 * 2**20
        ),
        name="exchange",
    )(matrix, panels)


def update_kernel(a_ref, x_ref, y_ref, o_ref, held, sems):
    copies = []
    for b in range(BLOCKS):
        columns = slice(b * SUBW, (b + 1) * SUBW)
        held[b] = (a_ref[b].astype(F32) - dot(x_ref[...], y_ref[:, columns], NN)).astype(BF16)
        copies.append(pltpu.make_async_copy(held.at[b], o_ref.at[:, pl.ds(b * SUBW, SUBW)], sems.at[b]))
        copies[b].start()
    for c in copies:
        c.wait()


def update(a, x, y):
    return pl.pallas_call(
        update_kernel,
        out_shape=jax.ShapeDtypeStruct((ROWS, 2 * ROWS), BF16),
        in_specs=[pl.BlockSpec(memory_space=pltpu.VMEM)] * 3,
        out_specs=pl.BlockSpec(memory_space=pl.ANY),
        scratch_shapes=[pltpu.VMEM((BLOCKS, ROWS, SUBW), BF16), pltpu.SemaphoreType.DMA((BLOCKS,))],
        compiler_params=pltpu.CompilerParams(vmem_limit_bytes=36 * 2**20),
        name="update",
    )(a, x, y)


def per_device(matrix, panels):
    return update(*exchange(matrix, panels))


def solution(mesh):
    return jax.shard_map(
        per_device,
        mesh=mesh,
        in_specs=(P("row", "col"), P(None, "row", None)),
        out_specs=P("row", "col"),
        check_vma=False,
    )
```

time: 571 us -> 57.8 us (0.10)
  waiting for transfers between devices: 345 us -> 0 us
  blocking collectives: 109 us -> 0 us
  matrix products: 69.1 us -> 0 us
  Pallas kernels: 0 us -> 56.5 us
  local copies, waits for them, and re-layouts: 26.3 us -> 1.13 us
  between operations: 13.6 us -> 0.01 us
    psum x2 -> x0, waiting for transfers between devices: 149 us -> none  [spread(): return lax.psum(block, axis)]
    reduce_scatter x2 -> x0, waiting for transfers between devices: 120 us -> none  [per_device(): lax.psum_scatter(lax.dot_general(tile_now, v_rows, (((0,), (0,)), ((), ()...]
    psum x2 -> x0, blocking collectives: 109 us -> none  [per_device(): lax.psum(local_sum.astype(jnp.bfloat16), 'row').astype(jnp.float32)]
    all_gather x4 -> x0, waiting for transfers between devices: 75 us -> none  [the longest x2 75 us: per_device(): av_cols = lax.all_gather(av_fine, 'row', axis=0, tiled=True)]
    dot_general x12 -> x0, matrix products: 69.1 us -> none  [the longest x2 29.3 us: per_device(): lax.dot_general(w_rows, v_cols, (((1,), (1,)), ((), ())), preferred_eleme...]
    pallas_call x0 -> x2, Pallas kernels: none -> 56.5 us  [the longest x1 50.3 us: exchange(): pl.pallas_call(exchange_kernel, out_shape=(jax.ShapeDtypeStruct((BLOCKS,...]
    convert_element_type x1 -> x0, local copies, waits for them, and re-layouts: 12.6 us -> none  [per_device(): a_tile = (a_tile.astype(jnp.float32) - update).astype(jnp.bfloat16)]
    unnamed x7 -> x2, local copies, waits for them, and re-layouts: 12.7 us -> 1.13 us
  transfers between devices with their start and end apart: 8 -> 0, of which waited for: 6 -> 0; matrix products, arithmetic and copies ran while one was open for 3% -> 0% of each run, Pallas kernels for 0% -> 0%
where the time goes in v2:
time: 57.8 us; the launch traced here: 57.7 us
  Pallas kernels  56.5 us (98%)
  local copies, waits for them, and re-layouts  1.13 us (2%)
    pallas_call x1, Pallas kernels, exchange(): pl.pallas_call(exchange_kernel, out_shape=(jax.ShapeDtypeStruct((BLOCKS,...  50.3 us
    pallas_call x1, Pallas kernels, update(): pl.pallas_call(update_kernel, out_shape=jax.ShapeDtypeStruct((ROWS, 2 * R...  6.27 us

profile of v2, /device:TPU:1, one launch (start us, length us, event | category | flops | bytes accessed | tf_op | source)
XLA Modules:
  0.0 57.7 jit_solution(5732942274022376881)
XLA Ops:
  0.0 0.0 copy-start
  0.0 1.1 %copy-done = bf16[2,1536,128]{2,1,0:T(8,128)(2,1)S(1)} copy-done((bf16[2,1536,128]{2,1,0:T(8,128)(2,1)S(1)}, bf16[2,1536,128]{2,1,0:T(8,128)(2,1)}, u32[]{:S(2)}) %copy-start) | copy-done | bytes 786456
  1.1 50.3 %exchange.1 = (bf16[6,1536,512]{2,1,0:T(8,128)(2,1)S(1)}, bf16[1536,512]{1,0:T(8,128)(2,1)S(1)}, bf16[512,3072]{1,0:T(8,128)(2,1)S(1)}) custom-call(bf16[1536,3072]{1,0:T(8,128)(2,1)} %a_ref.1, bf16[2,1536,128]{2,1,0:T(8,128)(2,1)S(1)} %copy-done), custom_call_target="tpu_custom_call" | custom-call | tf_op jit(solution)/shard_map/exchange/pallas_call | solution.py:295
  51.4 6.3 %update.1 = bf16[1536,3072]{1,0:T(8,128)(2,1)} custom-call(bf16[6,1536,512]{2,1,0:T(8,128)(2,1)S(1)} %get-tuple-element.8.a_ref, bf16[1536,512]{1,0:T(8,128)(2,1)S(1)} %get-tuple-element.9.x_ref, bf16[512,3072]{1,0:T(8,128)(2,1)S(1)} %get-tuple-element.10.y_ref), custom_call_target="tpu_custom_call" | custom-call | tf_op jit(solution)/shard_map/update/pallas_call | solution.py:344
Async XLA Ops:
  0.0 1.1 %copy-start = (bf16[2,1536,128]{2,1,0:T(8,128)(2,1)S(1)}, bf16[2,1536,128]{2,1,0:T(8,128)(2,1)}, u32[]{:S(2)}) copy-start(bf16[2,1536,128]{2,1,0:T(8,128)(2,1)} %v_ref.1) | copy-start | bytes 2359300

commit v3 on v2

v3 whole, which is shorter than its diff:
```python
import jax
import jax.numpy as jnp
from jax import lax
from jax.experimental import pallas as pl
from jax.experimental.pallas import tpu as pltpu
from jax.sharding import PartitionSpec as P

MESH = pl.DeviceIdType.MESH
F32 = jnp.float32
BF16 = jnp.bfloat16

ROWS = 1536
WIDE = 256
SUB = 3
SUBW = ROWS // SUB
BLOCKS = 2 * SUB
PIECE = 32
Z_FIRST = ()
AHEAD = 6
NN = (((1,), (0,)), ((), ()))
NT = (((1,), (1,)), ((), ()))


def dot(a, b, dims, precision=None):
    return lax.dot_general(a, b, dims, preferred_element_type=F32, precision=precision)


def exchange_kernel(
    a_ref, v_hbm, x_ref, y_ref, a_out,
    v_ref, vt, q_send, q_own, sib_in, x_send, x_in, z_send, z_in, zz_in, xx_send, xx_in,
    prt, g_send, g_in, g_full, c_send, c_row, c_full, c_sib,
    a_sem, s_send, s_recv,
):
    row = lax.axis_index("row")
    col = lax.axis_index("col")
    core = row % 2
    big = row // 2
    z = big % 4
    xl = big // 4
    yy = col % 4
    xh = col // 4

    sibling = (big * 2 + 1 - core, col)
    x_peer = (((1 - xl) * 4 + z) * 2 + core, col)
    z_peers = [((xl * 4 + (z + j) % 4) * 2 + core, col) for j in range(1, 4)]
    h_peer = (row, (1 - xh) * 4 + yy)
    y_peers = [(row, xh * 4 + (yy + j) % 4) for j in range(1, 4)]
    row_peers = [x_peer] + z_peers + [(((1 - xl) * 4 + (z + j) % 4) * 2 + core, col) for j in range(1, 4)]
    col_peers = [h_peer] + y_peers + [(row, (1 - xh) * 4 + (yy + j) % 4) for j in range(1, 4)]
    mirror = (col * 2 + core, big)
    on_diagonal = big == col
    off_diagonal = jnp.logical_not(on_diagonal)

    used = [0]
    sent = []

    def copy(src, dst, to):
        i = used[0]
        used[0] += 1
        return pltpu.make_async_remote_copy(
            src_ref=src, dst_ref=dst, send_sem=s_send.at[i], recv_sem=s_recv.at[i],
            device_id=to, device_id_type=MESH,
        )

    def send(src, dst, to):
        c = copy(src, dst, to)
        c.start()
        sent.append(c)
        return c

    panel_load = pltpu.make_async_copy(v_hbm, v_ref, a_sem.at[BLOCKS])
    panel_load.start()
    loads = []
    for i in range(BLOCKS):
        b = (1 - core if i % 2 == 0 else core) * SUB + i // 2
        start = pl.multiple_of(b * SUBW, 128)
        loads.append((b, pltpu.make_async_copy(a_ref.at[:, pl.ds(start, SUBW)], a_out.at[b], a_sem.at[i])))
    for _, load in loads[:AHEAD]:
        load.start()

    barrier = pltpu.get_barrier_semaphore()
    for peer in [sibling] + row_peers + col_peers:
        pl.semaphore_signal(barrier, inc=1, device_id=peer, device_id_type=MESH)

    @pl.when(off_diagonal)
    def _():
        pl.semaphore_signal(barrier, inc=1, device_id=mirror, device_id_type=MESH)

    panel_load.wait()
    vt[:128, :] = v_ref[0].T
    vt[128:, :] = v_ref[1].T
    g_send[0] = dot(vt[pl.ds(pl.multiple_of(col * 16, 16), 16), :], vt[128:, :], NT)

    mine = pl.multiple_of(big * PIECE, PIECE)
    mine_v = pl.multiple_of(WIDE + big * PIECE, PIECE)
    mine_r = pl.multiple_of(col * PIECE, PIECE)
    half = pl.multiple_of(core * ROWS, ROWS)

    def columns(s):
        return pl.ds(pl.multiple_of(core * ROWS + s * SUBW, 128), SUBW)

    v_turn = copy(
        vt.at[pl.ds(mine_r, PIECE)],
        y_ref.at[pl.ds(pl.multiple_of(WIDE + col * PIECE, PIECE), PIECE), pl.ds(half, ROWS)],
        mirror,
    )
    sib = []
    xs = [None] * SUB
    zs = [None] * SUB

    def reduce_first(s):
        sib[s].wait_recv()
        if s in Z_FIRST:
            total = q_own[s] + sib_in[s].astype(F32)
            q_own[s] = total
            z_send[s] = total.astype(BF16)
            zs[s] = [send(z_send.at[s, :, (z + j) % 4], zz_in.at[s, j - 1], z_peers[j - 1]) for j in range(1, 4)]
        else:
            x_send[s] = (q_own[s, 1 - xl] + sib_in[s, 1 - xl].astype(F32)).astype(BF16)
            xs[s] = send(x_send.at[s], x_in.at[s], x_peer)
            q_own[s, xl] = q_own[s, xl] + sib_in[s, xl].astype(F32)

    def reduce_second(s):
        if s in Z_FIRST:
            for c in zs[s]:
                c.wait_recv()
            total = q_own[s, :, z]
            for j in range(3):
                total = total + zz_in[s, j].astype(F32)
            q_own[s, :, z] = total
            xx_send[s] = q_own[s, 1 - xl, z].astype(BF16)
            xs[s] = send(xx_send.at[s], xx_in.at[s], x_peer)
        else:
            xs[s].wait_recv()
            total = q_own[s, xl] + x_in[s].astype(F32)
            q_own[s, xl] = total
            z_send[s, 0] = total.astype(BF16)
            zs[s] = [send(z_send.at[s, 0, (z + j) % 4], z_in.at[s, j - 1], z_peers[j - 1]) for j in range(1, 4)]

    turns = [None] * SUB
    p_x = [None] * SUB
    p_wait = [[] for _ in range(SUB)]

    def reduce_last(s):
        if s in Z_FIRST:
            xs[s].wait_recv()
            total = q_own[s, xl, z] + xx_in[s].astype(F32)
        else:
            total = q_own[s, xl, z]
            for j in range(3):
                zs[s][j].wait_recv()
                total = total + z_in[s, j].astype(F32)
        place = y_ref.at[pl.ds(mine, PIECE), columns(s)]
        place[...] = total.astype(BF16)
        turn = copy(place, prt.at[pl.ds(mine, PIECE), pl.ds(s * SUBW, SUBW)], mirror)
        turns[s] = turn

        @pl.when(off_diagonal)
        def _():
            turn.start()

        @pl.when(on_diagonal)
        def _():
            prt[pl.ds(mine, PIECE), pl.ds(s * SUBW, SUBW)] = place[...]

        p_x[s] = send(place, place, x_peer)
        p_wait[s] += [send(place, place, p) for p in z_peers]

    for i, (b, load) in enumerate(loads):
        load.wait()
        if i + AHEAD < BLOCKS:
            loads[i + AHEAD][1].start()
        part = dot(vt[...], a_out[b], NN).reshape(2, 4, PIECE, SUBW)
        if i % 2 == 0:
            q_send[i // 2] = part.astype(BF16)
        else:
            q_own[i // 2] = part
        if i == 1:

            @pl.when(on_diagonal)
            def _():
                pl.semaphore_wait(barrier, 15)
                y_ref[pl.ds(mine_v, PIECE), pl.ds(half, ROWS)] = vt[pl.ds(mine_r, PIECE), :]

            @pl.when(off_diagonal)
            def _():
                pl.semaphore_wait(barrier, 16)
                v_turn.start()

            sib.append(send(q_send.at[0], sib_in.at[0], sibling))
            g_sib = send(g_send.at[0], g_in.at[7], sibling)
        if i == 2 or i == 4:
            sib.append(send(q_send.at[i // 2], sib_in.at[i // 2], sibling))
        if i == 2:
            reduce_first(0)
        if i == 4:
            g_sib.wait_recv()
            g_send[1] = g_send[0] + g_in[7]
            gr = [send(g_send.at[1], g_in.at[j], p) for j, p in enumerate(row_peers)]
        if i == 4:
            reduce_first(1)
    reduce_first(2)

    @pl.when(off_diagonal)
    def _():
        v_turn.wait()

    v_place = y_ref.at[pl.ds(mine_v, PIECE), pl.ds(half, ROWS)]
    v_x = send(v_place, v_place, x_peer)
    v_wait = [send(v_place, v_place, p) for p in z_peers]
    total = g_send[1]
    for j in range(7):
        gr[j].wait_recv()
        total = total + g_in[j]
    place = g_full.at[pl.ds(pl.multiple_of(col * 16, 16), 16)]
    place[...] = total
    gc = [send(place, place, p) for p in col_peers]
    reduce_second(0)
    reduce_second(1)
    reduce_second(2)
    reduce_last(0)
    reduce_last(1)
    reduce_last(2)

    r_x = []
    r_wait = [[] for _ in range(SUB)]
    for s in range(SUB):

        @pl.when(off_diagonal)
        def _():
            turns[s].wait()

        place = prt.at[pl.ds(mine_r, PIECE), pl.ds(s * SUBW, SUBW)]
        r_x.append(send(place, place, h_peer))
        r_wait[s] += [send(place, place, p) for p in y_peers]
        part = dot(place[...], vt[:, s * SUBW:(s + 1) * SUBW], NT)
        if s == 0:
            c_send[...] = part
        else:
            c_send[...] = c_send[...] + part
    c_full[16] = c_send[...].astype(BF16)
    cr = [send(c_full.at[16], c_row.at[j], p) for j, p in enumerate(row_peers)]
    for c in v_wait:
        c.wait_recv()
    place = y_ref.at[pl.ds(pl.multiple_of(WIDE + xl * 128, 128), 128), pl.ds(half, ROWS)]
    v_share = [send(place, place, sibling)]

    other_p = pl.multiple_of(((1 - xl) * 4 + z) * PIECE, PIECE)
    for s in range(SUB):
        p_x[s].wait_recv()
        place = y_ref.at[pl.ds(other_p, PIECE), columns(s)]
        p_wait[s] += [send(place, place, p) for p in z_peers]

    total = c_send[...]
    for j in range(7):
        cr[j].wait_recv()
        total = total + c_row[j].astype(F32)
    place = c_full.at[core * 8 + col]
    place[...] = total.astype(BF16)
    cc = [send(place, place, p) for p in col_peers]

    other_r = pl.multiple_of(((1 - xh) * 4 + yy) * PIECE, PIECE)
    for s in range(SUB):
        r_x[s].wait_recv()
        place = prt.at[pl.ds(other_r, PIECE), pl.ds(s * SUBW, SUBW)]
        r_wait[s] += [send(place, place, p) for p in y_peers]

    v_x.wait_recv()
    place = y_ref.at[
        pl.ds(pl.multiple_of(WIDE + ((1 - xl) * 4 + z) * PIECE, PIECE), PIECE), pl.ds(half, ROWS)
    ]
    v_wait = [send(place, place, p) for p in z_peers]

    for c in gc:
        c.wait_recv()
    g01 = g_full[...]
    g01b = g01.astype(BF16)
    for s in range(SUB):
        rows = slice(s * SUBW, (s + 1) * SUBW)
        v1 = v_ref[1, rows]
        x_ref[rows, :128] = (v_ref[0, rows].astype(F32) - dot(v1, g01b, NT)).astype(BF16)
        x_ref[rows, 128:256] = v1

    for c in cc:
        c.wait_recv()
    place = c_full.at[pl.ds(pl.multiple_of(core * 8, 8), 8)]
    c_share = send(place, c_sib, sibling)
    c_share.wait_recv()

    cpv = jnp.concatenate([c_full[core * 8 + i].astype(F32) + c_sib[i].astype(F32) for i in range(8)], axis=0)
    cs = jnp.concatenate(
        [cpv[:, :128], cpv[:, 128:] - dot(cpv[:, :128], g01, NN, lax.Precision.HIGHEST)], axis=1
    ).astype(BF16)

    p_share = []
    for s in range(SUB):
        for c in p_wait[s]:
            c.wait_recv()
        place = y_ref.at[pl.ds(0, WIDE), columns(s)]
        p_share.append(send(place, place, sibling))

    for c in v_wait:
        c.wait_recv()
    place = y_ref.at[pl.ds(pl.multiple_of(WIDE + (1 - xl) * 128, 128), 128), pl.ds(half, ROWS)]
    v_share.append(send(place, place, sibling))

    for s in range(SUB):
        rows = slice(s * SUBW, (s + 1) * SUBW)
        vc = dot(x_ref[rows, :256], cs, NN)
        for c in r_wait[s]:
            c.wait_recv()
        p0 = prt[:128, rows].T
        p1 = prt[128:, rows].T
        x_ref[rows, 256:384] = (p0.astype(F32) - vc[:, :128]).astype(BF16)
        x_ref[rows, 384:] = (p1.astype(F32) - dot(p0, g01b, NN) - vc[:, 128:]).astype(BF16)

    for c in v_share + p_share:
        c.wait_recv()
    for c in sent:
        c.wait_send()


N_COPIES = 128


def exchange(matrix, panels):
    return pl.pallas_call(
        exchange_kernel,
        out_shape=(
            jax.ShapeDtypeStruct((ROWS, 2 * WIDE), BF16),
            jax.ShapeDtypeStruct((2 * WIDE, 2 * ROWS), BF16),
            jax.ShapeDtypeStruct((BLOCKS, ROWS, SUBW), BF16),
        ),
        in_specs=[pl.BlockSpec(memory_space=pltpu.HBM)] * 2,
        out_specs=(pl.BlockSpec(memory_space=pltpu.VMEM),) * 3,
        scratch_shapes=[
            pltpu.VMEM((2, ROWS, WIDE // 2), BF16),
            pltpu.VMEM((WIDE, ROWS), BF16),
            pltpu.VMEM((SUB, 2, 4, PIECE, SUBW), BF16),
            pltpu.VMEM((SUB, 2, 4, PIECE, SUBW), F32),
            pltpu.VMEM((SUB, 2, 4, PIECE, SUBW), BF16),
            pltpu.VMEM((SUB, 4, PIECE, SUBW), BF16),
            pltpu.VMEM((SUB, 4, PIECE, SUBW), BF16),
            pltpu.VMEM((SUB, 2, 4, PIECE, SUBW), BF16),
            pltpu.VMEM((SUB, 3, PIECE, SUBW), BF16),
            pltpu.VMEM((SUB, 3, 2, PIECE, SUBW), BF16),
            pltpu.VMEM((SUB, PIECE, SUBW), BF16),
            pltpu.VMEM((SUB, PIECE, SUBW), BF16),
            pltpu.VMEM((WIDE, ROWS), BF16),
            pltpu.VMEM((2, 16, 128), F32),
            pltpu.VMEM((8, 16, 128), F32),
            pltpu.VMEM((128, 128), F32),
            pltpu.VMEM((PIECE, WIDE), F32),
            pltpu.VMEM((7, PIECE, WIDE), BF16),
            pltpu.VMEM((17, PIECE, WIDE), BF16),
            pltpu.VMEM((8, PIECE, WIDE), BF16),
            pltpu.SemaphoreType.DMA((BLOCKS + 1,)),
            pltpu.SemaphoreType.DMA((N_COPIES,)),
            pltpu.SemaphoreType.DMA((N_COPIES,)),
        ],
        compiler_params=pltpu.CompilerParams(
            collective_id=0, has_side_effects=True, vmem_limit_bytes=36 * 2**20
        ),
        name="exchange",
    )(matrix, panels)


def update_kernel(x_ref, y_ref, a_ref, o_ref, held, sems):
    copies = []
    parts = [(b, 0, ROWS) for b in range(BLOCKS - 1)] + [(BLOCKS - 1, i * ROWS // 3, ROWS // 3) for i in range(3)]
    for i, (b, start, count) in enumerate(parts):
        columns = slice(b * SUBW, (b + 1) * SUBW)
        rows = slice(start, start + count)
        held[b, rows] = (a_ref[b, rows].astype(F32) - dot(x_ref[rows], y_ref[:, columns], NN)).astype(BF16)
        copies.append(
            pltpu.make_async_copy(
                held.at[b, pl.ds(start, count)], o_ref.at[pl.ds(start, count), pl.ds(b * SUBW, SUBW)], sems.at[i]
            )
        )
        copies[i].start()
    for c in copies:
        c.wait()


def update(x, y, a):
    return pl.pallas_call(
        update_kernel,
        out_shape=jax.ShapeDtypeStruct((ROWS, 2 * ROWS), BF16),
        in_specs=[pl.BlockSpec(memory_space=pltpu.VMEM)] * 3,
        out_specs=pl.BlockSpec(memory_space=pl.ANY),
        scratch_shapes=[pltpu.VMEM((BLOCKS, ROWS, SUBW), BF16), pltpu.SemaphoreType.DMA((BLOCKS + 2,))],
        compiler_params=pltpu.CompilerParams(vmem_limit_bytes=36 * 2**20),
        name="update",
    )(x, y, a)


def per_device(matrix, panels):
    panels = pltpu.with_memory_space_constraint(panels, pltpu.HBM)
    return update(*exchange(matrix, panels))


def solution(mesh):
    return jax.shard_map(
        per_device,
        mesh=mesh,
        in_specs=(P("row", "col"), P(None, "row", None)),
        out_specs=P("row", "col"),
        check_vma=False,
    )
```

time: 57.8 us -> 55.6 us (0.962)
  local copies, waits for them, and re-layouts: 1.13 us -> 0 us
  Pallas kernels: 56.5 us -> 55.5 us
    unnamed x2 -> x0, local copies, waits for them, and re-layouts: 1.13 us -> none
    pallas_call x1, Pallas kernels: 50.3 us -> 49.6 us  [exchange(): pl.pallas_call(exchange_kernel, out_shape=(jax.ShapeDtypeStruct((ROWS, 2...]
where the time goes in v3:
time: 55.6 us; the launch traced here: 55.5 us
  Pallas kernels  55.5 us (100%)
    pallas_call x1, Pallas kernels, exchange(): pl.pallas_call(exchange_kernel, out_shape=(jax.ShapeDtypeStruct((ROWS, 2...  49.6 us
    pallas_call x1, Pallas kernels, update(): pl.pallas_call(update_kernel, out_shape=jax.ShapeDtypeStruct((ROWS, 2 * R...  5.95 us

profile of v3, /device:TPU:1, one launch (start us, length us, event | category | flops | bytes accessed | tf_op | source)
XLA Modules:
  0.0 55.5 jit_solution(5000063589295715018)
XLA Ops:
  0.0 49.6 %exchange.1 = (bf16[1536,512]{1,0:T(8,128)(2,1)S(1)}, bf16[512,3072]{1,0:T(8,128)(2,1)S(1)}, bf16[6,1536,512]{2,1,0:T(8,128)(2,1)S(1)}) custom-call(bf16[1536,3072]{1,0:T(8,128)(2,1)} %a_ref.1, bf16[2,1536,128]{2,1,0:T(8,128)(2,1)} %v_hbm.1), custom_call_target="tpu_custom_call" | custom-call | tf_op jit(solution)/shard_map/exchange/pallas_call | solution.py:327
  49.6 5.9 %update.1 = bf16[1536,3072]{1,0:T(8,128)(2,1)} custom-call(bf16[1536,512]{1,0:T(8,128)(2,1)S(1)} %get-tuple-element.8.x_ref, bf16[512,3072]{1,0:T(8,128)(2,1)S(1)} %get-tuple-element.9.y_ref, bf16[6,1536,512]{2,1,0:T(8,128)(2,1)S(1)} %get-tuple-element.10.a_ref), custom_call_target="tpu_custom_call" | custom-call | tf_op jit(solution)/shard_map/update/pallas_call | solution.py:386

commit v4 on v3

--- a/solution.py
+++ b/solution.py
@@ -208,6 +208,9 @@
     v_place = y_ref.at[pl.ds(mine_v, PIECE), pl.ds(half, ROWS)]
     v_x = send(v_place, v_place, x_peer)
     v_wait = [send(v_place, v_place, p) for p in z_peers]
+    reduce_second(0)
+    reduce_second(1)
+    reduce_second(2)
     total = g_send[1]
     for j in range(7):
         gr[j].wait_recv()
@@ -215,9 +218,6 @@
     place = g_full.at[pl.ds(pl.multiple_of(col * 16, 16), 16)]
     place[...] = total
     gc = [send(place, place, p) for p in col_peers]
-    reduce_second(0)
-    reduce_second(1)
-    reduce_second(2)
     reduce_last(0)
     reduce_last(1)
     reduce_last(2)
@@ -273,8 +273,7 @@
 
     for c in gc:
         c.wait_recv()
-    g01 = g_full[...]
-    g01b = g01.astype(BF16)
+    g01b = g_full[...].astype(BF16)
     for s in range(SUB):
         rows = slice(s * SUBW, (s + 1) * SUBW)
         v1 = v_ref[1, rows]
@@ -287,9 +286,8 @@
     c_share = send(place, c_sib, sibling)
     c_share.wait_recv()
 
-    cpv = jnp.concatenate([c_full[core * 8 + i].astype(F32) + c_sib[i].astype(F32) for i in range(8)], axis=0)
-    cs = jnp.concatenate(
-        [cpv[:, :128], cpv[:, 128:] - dot(cpv[:, :128], g01, NN, lax.Precision.HIGHEST)], axis=1
+    curvature = jnp.concatenate(
+        [c_full[core * 8 + i].astype(F32) + c_sib[i].astype(F32) for i in range(8)], axis=0
     ).astype(BF16)
 
     p_share = []
@@ -299,20 +297,22 @@
         place = y_ref.at[pl.ds(0, WIDE), columns(s)]
         p_share.append(send(place, place, sibling))
 
-    for c in v_wait:
-        c.wait_recv()
-    place = y_ref.at[pl.ds(pl.multiple_of(WIDE + (1 - xl) * 128, 128), 128), pl.ds(half, ROWS)]
-    v_share.append(send(place, place, sibling))
 
     for s in range(SUB):
         rows = slice(s * SUBW, (s + 1) * SUBW)
-        vc = dot(x_ref[rows, :256], cs, NN)
+        vc = dot(x_ref[rows, :256], curvature, NN)
         for c in r_wait[s]:
             c.wait_recv()
         p0 = prt[:128, rows].T
         p1 = prt[128:, rows].T
-        x_ref[rows, 256:384] = (p0.astype(F32) - vc[:, :128]).astype(BF16)
-        x_ref[rows, 384:] = (p1.astype(F32) - dot(p0, g01b, NN) - vc[:, 128:]).astype(BF16)
+        first = (p0.astype(F32) - vc[:, :128]).astype(BF16)
+        x_ref[rows, 256:384] = first
+        x_ref[rows, 384:] = (p1.astype(F32) - vc[:, 128:] - dot(first, g01b, NN)).astype(BF16)
+        if s == 0:
+            for c in v_wait:
+                c.wait_recv()
+            place = y_ref.at[pl.ds(pl.multiple_of(WIDE + (1 - xl) * 128, 128), 128), pl.ds(half, ROWS)]
+            v_share.append(send(place, place, sibling))
 
     for c in v_share + p_share:
         c.wait_recv()

time: 55.6 us -> 55.6 us (level)
  no operation moved by 1% of the time
where the time goes in v4:
time: 55.6 us; the launch traced here: 55.5 us
  Pallas kernels  55.5 us (100%)
    pallas_call x1, Pallas kernels, exchange(): pl.pallas_call(exchange_kernel, out_shape=(jax.ShapeDtypeStruct((ROWS, 2...  49.6 us
    pallas_call x1, Pallas kernels, update(): pl.pallas_call(update_kernel, out_shape=jax.ShapeDtypeStruct((ROWS, 2 * R...  5.94 us

profile of v4, /device:TPU:1, one launch (start us, length us, event | category | flops | bytes accessed | tf_op | source)
XLA Modules:
  0.0 55.5 jit_solution(2015300553289252994)
XLA Ops:
  0.0 49.6 %exchange.1 = (bf16[1536,512]{1,0:T(8,128)(2,1)S(1)}, bf16[512,3072]{1,0:T(8,128)(2,1)S(1)}, bf16[6,1536,512]{2,1,0:T(8,128)(2,1)S(1)}) custom-call(bf16[1536,3072]{1,0:T(8,128)(2,1)} %a_ref.1, bf16[2,1536,128]{2,1,0:T(8,128)(2,1)} %v_hbm.1), custom_call_target="tpu_custom_call" | custom-call | tf_op jit(solution)/shard_map/exchange/pallas_call | solution.py:327
  49.6 5.9 %update.1 = bf16[1536,3072]{1,0:T(8,128)(2,1)} custom-call(bf16[1536,512]{1,0:T(8,128)(2,1)S(1)} %get-tuple-element.8.x_ref, bf16[512,3072]{1,0:T(8,128)(2,1)S(1)} %get-tuple-element.9.y_ref, bf16[6,1536,512]{2,1,0:T(8,128)(2,1)S(1)} %get-tuple-element.10.a_ref), custom_call_target="tpu_custom_call" | custom-call | tf_op jit(solution)/shard_map/update/pallas_call | solution.py:386
